TPU v7x, 512 devices: a whole 4x8x8 slice. The times are simulated.
512 devices in a mesh: space: 8 (over z), vel: 64 (over x, y, core).
Axes of the slice: x: 4, y: 8, z: 8, core: 2. Of those that a mesh axis runs over, the one named last changes fastest.
Arguments:
- distribution: float32 [32768, 2048], P('vel', 'space'), may hold values from 0.1 to 32, as said below
- normals: float32 [4, 3, 2048], P(None, None, 'space'), may hold values from -0.3 to 0.3
- adjacency: int32 [4, 2048], P(None, 'space'), may hold values from 0 to 2047, as said below
- send_list: int32 [8, 8, 256], P('space'), may hold values from 0 to 255
- block_counts: int32 [8, 8], P(None, 'space'), may hold values from 0 to 2, as said below
Outputs:
- relaxed: float32 [32768, 2048], P('vel', 'space')
- fields: float32 [13, 2048], P(None, 'space')
Inputs may be any that keep to these rules, and one draw needn't show every extreme that they name: `adjacency`: every entry of 256 or more names a position below 128 times the sum of block_counts over the senders to its group. `block_counts`: no group sends to itself; every other pair has at least one block; one receiving group gets 2 blocks from every other group. `distribution`: Positive.
All inputs are finite; a program needn't handle non-finite values.
Results may differ from a plain program's by a relative error of at most 0.00011.
Values sent between devices are 32-bit elements; how exact they have to be, the bound alone decides.
No kernel may reach another device: no remote copies, remote signals or barrier semaphores. Data moves between devices by JAX's collectives and lax.ppermute only.
A program may use at most 64 MiB of HBM per device.

v0:
```python
import jax
import jax.numpy as jnp
from jax import lax
from jax.sharding import PartitionSpec as P

VXY = 32
TILE = 128
BND = 256
ITERS = 2
spacing = 0.3
ellipsoid_mix = -0.25
prandtl = 0.8
visc_power = 0.26
time_step = 0.025


def sent_to_all(x, axis):
    copies = jnp.broadcast_to(x, (lax.axis_size(axis), *x.shape))
    return lax.all_to_all(copies, axis, split_axis=0, concat_axis=0, tiled=True)


def laid_out(pieces, dim):
    pieces = jnp.moveaxis(pieces, 0, dim)
    shape = pieces.shape
    return pieces.reshape(*shape[:dim], shape[dim] * shape[dim + 1], *shape[dim + 2 :])


def gather_directly(x, axis, dim):
    pieces = sent_to_all(x, axis)
    return laid_out(pieces, dim)


def of_everyone(x, axis):
    return sent_to_all(x, axis).sum(axis=0)


def velocity_nodes(vel_index, z_count):
    comp_x = (vel_index % VXY).astype(jnp.float32)
    comp_y = (vel_index // VXY % VXY).astype(jnp.float32)
    comp_z = (vel_index // (VXY * VXY)).astype(jnp.float32)
    centre = (VXY - 1) / 2.0
    return jnp.stack(
        [
            (comp_x - centre) * spacing,
            (comp_y - centre) * spacing,
            (comp_z - (z_count - 1) / 2.0) * spacing,
        ]
    )


def moment_rows(velocity):
    comp_x, comp_y, comp_z = (velocity[0], velocity[1], velocity[2])
    squared = comp_x * comp_x + comp_y * comp_y + comp_z * comp_z
    return jnp.stack(
        [
            jnp.ones_like(comp_x),
            comp_x,
            comp_y,
            comp_z,
            comp_x * comp_x,
            comp_y * comp_y,
            comp_z * comp_z,
            comp_x * comp_y,
            comp_x * comp_z,
            comp_y * comp_z,
            comp_x * squared,
            comp_y * squared,
            comp_z * squared,
        ]
    )


def quad_rows(velocity):
    comp_x, comp_y, comp_z = (velocity[0], velocity[1], velocity[2])
    return jnp.stack(
        [
            comp_x * comp_x,
            comp_y * comp_y,
            comp_z * comp_z,
            comp_x * comp_y,
            comp_x * comp_z,
            comp_y * comp_z,
            comp_x,
            comp_y,
            comp_z,
            jnp.ones_like(comp_x),
        ]
    )


def macroscopic(moments):
    density = moments[0]
    mean_x = moments[1] / density
    mean_y = moments[2] / density
    mean_z = moments[3] / density
    second = moments[4:10] / density[None, :]
    third = moments[10:13] / density[None, :]
    theta_xx = second[0] - mean_x * mean_x
    theta_yy = second[1] - mean_y * mean_y
    theta_zz = second[2] - mean_z * mean_z
    theta_xy = second[3] - mean_x * mean_y
    theta_xz = second[4] - mean_x * mean_z
    theta_yz = second[5] - mean_y * mean_z
    temper = (theta_xx + theta_yy + theta_zz) / 3.0
    trace_b = second[0] + second[1] + second[2]
    bu_x = second[0] * mean_x + second[3] * mean_y + second[4] * mean_z
    bu_y = second[3] * mean_x + second[1] * mean_y + second[5] * mean_z
    bu_z = second[4] * mean_x + second[5] * mean_y + second[2] * mean_z
    mean_sq = mean_x * mean_x + mean_y * mean_y + mean_z * mean_z
    flux_x = 0.5 * (third[0] - 2.0 * bu_x - mean_x * trace_b + 2.0 * mean_x * mean_sq)
    flux_y = 0.5 * (third[1] - 2.0 * bu_y - mean_y * trace_b + 2.0 * mean_y * mean_sq)
    flux_z = 0.5 * (third[2] - 2.0 * bu_z - mean_z * trace_b + 2.0 * mean_z * mean_sq)
    iso_part = (1.0 - ellipsoid_mix) * temper
    lam_xx = iso_part + ellipsoid_mix * theta_xx
    lam_yy = iso_part + ellipsoid_mix * theta_yy
    lam_zz = iso_part + ellipsoid_mix * theta_zz
    lam_xy = ellipsoid_mix * theta_xy
    lam_xz = ellipsoid_mix * theta_xz
    lam_yz = ellipsoid_mix * theta_yz
    cof_xx = lam_yy * lam_zz - lam_yz * lam_yz
    cof_xy = lam_yz * lam_xz - lam_xy * lam_zz
    cof_xz = lam_xy * lam_yz - lam_yy * lam_xz
    cof_yy = lam_xx * lam_zz - lam_xz * lam_xz
    cof_yz = lam_xy * lam_xz - lam_xx * lam_yz
    cof_zz = lam_xx * lam_yy - lam_xy * lam_xy
    determinant = lam_xx * cof_xx + lam_xy * cof_xy + lam_xz * cof_xz
    inv_xx = cof_xx / determinant
    inv_yy = cof_yy / determinant
    inv_zz = cof_zz / determinant
    inv_xy = cof_xy / determinant
    inv_xz = cof_xz / determinant
    inv_yz = cof_yz / determinant
    lin_x = inv_xx * mean_x + inv_xy * mean_y + inv_xz * mean_z
    lin_y = inv_xy * mean_x + inv_yy * mean_y + inv_yz * mean_z
    lin_z = inv_xz * mean_x + inv_yz * mean_y + inv_zz * mean_z
    offset = mean_x * lin_x + mean_y * lin_y + mean_z * lin_z
    collide = prandtl * density * jnp.exp(visc_power * jnp.log(temper))
    return jnp.stack(
        [
            density,
            mean_x,
            mean_y,
            mean_z,
            theta_xx,
            theta_yy,
            theta_zz,
            theta_xy,
            theta_xz,
            theta_yz,
            flux_x,
            flux_y,
            flux_z,
            inv_xx,
            inv_yy,
            inv_zz,
            2.0 * inv_xy,
            2.0 * inv_xz,
            2.0 * inv_yz,
            -2.0 * lin_x,
            -2.0 * lin_y,
            -2.0 * lin_z,
            offset,
            collide,
        ]
    )


def ghost_slots(adjacency, counts, cells, groups, slot_count):
    ends = jnp.cumsum(counts) * TILE
    starts = ends - counts * TILE
    is_local = adjacency < cells
    position = jnp.maximum(adjacency - cells, 0)
    source = jnp.sum((ends[:, None, None] <= position[None]).astype(jnp.int32), axis=0)
    source = jnp.minimum(source, groups - 1)
    group_ids = jnp.arange(groups, dtype=jnp.int32)[:, None, None]
    chosen = jnp.sum(jnp.where(group_ids == source[None], starts[:, None, None], 0), axis=0)
    slot_pos = jnp.clip(position - chosen, 0, slot_count - 1)
    return (is_local, source, slot_pos)


def relax(current, neighbours, velocity, normals, params, norm_z, equilibrium):
    gauss = params[0][None, :] * equilibrium / norm_z[None, :]
    outflow = jnp.zeros(current.shape, jnp.float32)
    inflow = jnp.zeros(current.shape, jnp.float32)
    for side in range(normals.shape[0]):
        normal_speed = (
            velocity[0][:, None] * normals[side, 0][None, :]
            + velocity[1][:, None] * normals[side, 1][None, :]
            + velocity[2][:, None] * normals[side, 2][None, :]
        )
        outflow = outflow + jnp.maximum(normal_speed, 0.0)
        inflow = inflow + jnp.minimum(normal_speed, 0.0) * neighbours[side]
    return current + time_step * (
        params[23][None, :] * (gauss - current) - outflow * current - inflow
    )


def per_device(distribution, normals, adjacency, send_list, block_counts):
    vel_local = distribution.shape[0]
    cells = distribution.shape[1]
    total_vel = vel_local * lax.axis_size("vel")
    z_count = total_vel // (VXY * VXY)
    groups = send_list.shape[1]
    slot_count = send_list.shape[2]
    vel_index = lax.axis_index("vel") * vel_local + jnp.arange(vel_local, dtype=jnp.int32)
    velocity = velocity_nodes(vel_index, z_count)
    moment_table = moment_rows(velocity)
    quad_table = quad_rows(velocity).T
    is_local, source, slot_pos = ghost_slots(
        adjacency, block_counts[:, 0], cells, groups, slot_count
    )
    ghost_index = source * slot_count + slot_pos
    local_index = jnp.where(is_local, adjacency, 0)
    list_all = gather_directly(send_list, "space", 0)
    column = lax.dynamic_index_in_dim(list_all, lax.axis_index("space"), 1, keepdims=False)
    pull_index = (jnp.arange(groups, dtype=jnp.int32)[:, None] * BND + column).reshape(-1)

    def reduce_moments(current):
        partial_value = (
            jnp.dot(
                moment_table,
                current,
                precision=lax.Precision.HIGHEST,
                preferred_element_type=jnp.float32,
            )
            / total_vel
        )
        return macroscopic(of_everyone(partial_value, "vel"))

    current = distribution
    for iteration in range(ITERS):
        params = reduce_moments(current)
        border = lax.all_gather(current, "space", axis=1, tiled=True)
        ghosts = jnp.take(border, pull_index, axis=1)
        exponent = jnp.dot(
            quad_table,
            params[13:23],
            precision=lax.Precision.HIGHEST,
            preferred_element_type=jnp.float32,
        )
        equilibrium = jnp.exp(-0.5 * exponent)
        norm_z = of_everyone(jnp.sum(equilibrium, axis=0) / total_vel, "vel")
        neighbours = [
            jnp.where(
                is_local[side][None, :],
                jnp.take(current, local_index[side], axis=1),
                jnp.take(ghosts, ghost_index[side], axis=1),
            )
            for side in range(normals.shape[0])
        ]
        current = relax(current, neighbours, velocity, normals, params, norm_z, equilibrium)
    final = reduce_moments(current)
    return (current, final[:13])


def solution(mesh):
    placed = (
        P("vel", "space"),
        P(None, None, "space"),
        P(None, "space"),
        P("space", None, None),
        P(None, "space"),
    )
    return jax.shard_map(
        per_device,
        mesh=mesh,
        in_specs=placed,
        out_specs=(P("vel", "space"), P(None, "space")),
        check_vma=False,
    )
```

profile of v0, /device:TPU:1, one launch (start us, length us, event | category | flops | bytes accessed | tf_op | source)
XLA Modules:
  0.0 278.8 jit_solution(2723023578636813399)
XLA Ops:
  7.2 2.0 copy.61
  9.3 1.4 broadcast_in_dim.117
  10.7 10.9 %all-to-all-start.2 = ((s32[8,1,8,256]{3,2,1,0:T(8,128)}), s32[8,1,8,256]{3,2,1,0:T(8,128)S(1)}, u32[]{:S(2)}, u32[]{:S(2)}) async-start(s32[8,1,8,256]{3,2,1,0:T(8,128)} %broadcast_in_dim.117), calls=%async_computation.2 | async-start | bytes 131072 | tf_op jit(solution)/shard_map/all_to_all | solution.py:19
  21.5 0.8 reduce-window.7
  22.4 0.7 bitcast_subtract_fusion
  23.3 0.7 add_maximum_fusion
  24.2 0.7 broadcast_select_fusion
  25.3 0.7 broadcast_compare_fusion
  26.0 1.3 convolution_multiply_fusion.4
  27.5 1.0 gather_fusion.7
  28.5 0.2 copy.72
  28.7 1.0 gather_fusion.5
  29.6 0.2 copy.69
  29.8 1.0 gather_fusion.3
  31.0 1.0 gather_fusion
  32.0 0.2 copy.62
  32.2 1.1 broadcast_in_dim.112
  33.4 11.1 %all-to-all-start = ((f32[64,13,256]{2,1,0:T(8,128)}), f32[64,13,256]{2,1,0:T(8,128)S(1)}, u32[]{:S(2)}, u32[]{:S(2)}) async-start(f32[64,13,256]{2,1,0:T(8,128)} %broadcast_in_dim.112), calls=%async_computation | async-start | bytes 2097152 | tf_op jit(solution)/shard_map/all_to_all | solution.py:19
  44.6 28.4 %all-to-all-done = f32[64,13,256]{2,1,0:T(8,128)S(1)} async-done(((f32[64,13,256]{2,1,0:T(8,128)}), f32[64,13,256]{2,1,0:T(8,128)S(1)}, u32[]{:S(2)}, u32[]{:S(2)}) %all-to-all-start) | async-done | bytes 852000 | tf_op jit(solution)/shard_map/all_to_all | solution.py:19
  73.3 0.6 fusion.94
  74.0 0.7 broadcast_in_dim.113
  74.6 6.2 %all-to-all-start.1 = ((f32[64,1,256]{2,1,0:T(1,128)}), f32[64,1,256]{2,1,0:T(1,128)S(1)}, u32[]{:S(2)}, u32[]{:S(2)}) async-start(f32[64,1,256]{2,1,0:T(1,128)} %broadcast_in_dim.113), calls=%async_computation.1 | async-start | bytes 131072 | tf_op jit(solution)/shard_map/all_to_all | solution.py:19
  80.8 0.2 all-gather.5.cloned.1.call-start
  81.1 9.5 %all-to-all-done.1 = f32[64,1,256]{2,1,0:T(1,128)S(1)} async-done(((f32[64,1,256]{2,1,0:T(1,128)}), f32[64,1,256]{2,1,0:T(1,128)S(1)}, u32[]{:S(2)}, u32[]{:S(2)}) %all-to-all-start.1) | async-done | bytes 65568 | tf_op jit(solution)/shard_map/all_to_all | solution.py:19
  90.8 11.7 %gather_fusion.1 = f32[2048,512]{1,0:T(8,128)} fusion(f32[512,2048]{0,1:T(8,128)} %all-gather.3.cloned.1.call-done, s32[2048]{0:T(1024)S(1)} %broadcast_clamp_fusion), kind=kCustom, calls=%fused_computation.1.clone | custom fusion | bytes 8396800 | tf_op jit(solution)/shard_map/jit(_take)/gather | solution.py:234
  102.5 3.8 %select_bitcast_fusion.1 = f32[512,2048]{0,1:T(8,128)} fusion(f32[2048,512]{1,0:T(8,128)} %gather_fusion.1, pred[2048]{0:T(1024)(128)(4,1)S(1)} %compare_and_fusion), kind=kLoop, calls=%fused_computation.19 | loop fusion | flops 1048576 | bytes 8390656 | tf_op jit(solution)/shard_map/jit(_take)/select_n | solution.py:234
  106.3 3.4 %gather_fusion.8 = f32[256,512]{1,0:T(8,128)S(1)} fusion(f32[512,2048]{0,1:T(8,128)} %select_bitcast_fusion.1, s32[1024]{0:T(1024)S(1)} %pad_clamp_fusion), kind=kCustom, calls=%fused_computation.13.clone | custom fusion | bytes 1049600 | tf_op jit(solution)/shard_map/jit(_take)/gather | solution.py:247
  109.7 1.0 copy.73
  110.7 3.4 %gather_fusion.6 = f32[256,512]{1,0:T(8,128)S(1)} fusion(f32[512,2048]{0,1:T(8,128)} %select_bitcast_fusion.1, s32[1024]{0:T(1024)S(1)} %pad_clamp_fusion.2), kind=kCustom, calls=%fused_computation.12.clone | custom fusion | bytes 1049600 | tf_op jit(solution)/shard_map/jit(_take)/gather | solution.py:247
  114.1 1.0 copy.70
  115.1 4.2 %gather_fusion.4 = f32[256,512]{1,0:T(8,128)} fusion(f32[512,2048]{0,1:T(8,128)} %select_bitcast_fusion.1, s32[1024]{0:T(1024)S(1)} %pad_clamp_fusion.4), kind=kCustom, calls=%fused_computation.11.clone | custom fusion | bytes 1049600 | tf_op jit(solution)/shard_map/jit(_take)/gather | solution.py:247
  119.3 2.1 copy.67
  121.4 4.2 %gather_fusion.2 = f32[256,512]{1,0:T(8,128)} fusion(f32[512,2048]{0,1:T(8,128)} %select_bitcast_fusion.1, s32[1024]{0:T(1024)S(1)} %pad_clamp_fusion.6), kind=kCustom, calls=%fused_computation.2.clone | custom fusion | bytes 1049600 | tf_op jit(solution)/shard_map/jit(_take)/gather | solution.py:247
  125.6 2.1 copy.64
  127.6 3.6 %fusion.16 = f32[512,256]{1,0:T(8,128)} fusion(f32[512,256]{1,0:T(8,128)S(1)} %copy-done.2, f32[256,512]{0,1:T(8,128)} %copy.73, f32[256,512]{0,1:T(8,128)S(1)} %copy.72, f32[256,512]{0,1:T(8,128)} %copy.70, f32[256,512]{0,1:T(8,128)S(1)} %copy.69, f32[256,512]{0,1:T(8,128)} %copy.67, f32[256,512]{0,1:T(8,128)S(1)} %copy.66, f32[256,512]{0,1:T(8,128)} %copy.64, ...), kind=kLoop, calls=%fused_computation.46 | loop fusion | flops 7733248 | bytes 5791744 | tf_op jit(solution)/shard_map/add | solution.py:193
  131.2 1.4 convolution_multiply_fusion.3
  132.8 32.4 %all_to_all.32 = f32[64,13,256]{2,1,0:T(8,128)S(1)} all-to-all(f32[64,13,256]{2,1,0:T(8,128)S(1)} %broadcast_in_dim.126), channel_id=1, replica_groups=mesh['space'=8,'vel'=64] {'vel'}, dimensions={0} | all-to-all | bytes 1703936 | tf_op jit(solution)/shard_map/all_to_all | solution.py:19
  165.5 0.6 fusion.95
  166.2 0.7 broadcast_in_dim.127
  166.8 6.2 %all-to-all-start.4 = ((f32[64,1,256]{2,1,0:T(1,128)}), f32[64,1,256]{2,1,0:T(1,128)S(1)}, u32[]{:S(2)}, u32[]{:S(2)}) async-start(f32[64,1,256]{2,1,0:T(1,128)} %broadcast_in_dim.127), calls=%async_computation.4 | async-start | bytes 131072 | tf_op jit(solution)/shard_map/all_to_all | solution.py:19
  173.1 0.2 copy.76
  173.3 1.0 gather_fusion.16
  174.2 1.0 gather_fusion.14
  175.2 1.8 gather_fusion.12
  177.0 1.8 gather_fusion.9
  179.2 1.2 copy.81
  180.4 2.1 copy.77
  182.5 0.3 all-to-all-done.4
  182.9 1.5 all-gather.5.cloned.1.call-done
  184.5 5.3 %copy.78 = f32[512,2048]{0,1:T(8,128)} copy(f32[512,2048]{1,0:T(8,128)} %all-gather.5.cloned.1.call-done) | data formatting | bytes 8388608 | tf_op jit(solution)/shard_map/all_gather | solution.py:233
  189.8 11.7 %gather_fusion.10 = f32[2048,512]{1,0:T(8,128)} fusion(f32[512,2048]{0,1:T(8,128)} %copy.78, s32[2048]{0:T(1024)S(1)} %broadcast_clamp_fusion), kind=kCustom, calls=%fused_computation.10.clone | custom fusion | bytes 8396800 | tf_op jit(solution)/shard_map/jit(_take)/gather | solution.py:234
  201.5 3.7 %select_bitcast_fusion = f32[512,2048]{0,1:T(8,128)} fusion(f32[2048,512]{1,0:T(8,128)} %gather_fusion.10, pred[2048]{0:T(1024)(128)(4,1)S(1)} %compare_and_fusion), kind=kLoop, calls=%fused_computation.18 | loop fusion | flops 1048576 | bytes 8390656 | tf_op jit(solution)/shard_map/jit(_take)/select_n | solution.py:234
  205.3 3.4 %gather_fusion.17 = f32[256,512]{1,0:T(8,128)S(1)} fusion(f32[512,2048]{0,1:T(8,128)} %select_bitcast_fusion, s32[1024]{0:T(1024)S(1)} %pad_clamp_fusion), kind=kCustom, calls=%fused_computation.17.clone | custom fusion | bytes 1049600 | tf_op jit(solution)/shard_map/jit(_take)/gather | solution.py:247
  208.7 4.2 %gather_fusion.15 = f32[256,512]{1,0:T(8,128)} fusion(f32[512,2048]{0,1:T(8,128)} %select_bitcast_fusion, s32[1024]{0:T(1024)S(1)} %pad_clamp_fusion.2), kind=kCustom, calls=%fused_computation.16.clone | custom fusion | bytes 1049600 | tf_op jit(solution)/shard_map/jit(_take)/gather | solution.py:247
  212.9 4.2 %gather_fusion.13 = f32[256,512]{1,0:T(8,128)} fusion(f32[512,2048]{0,1:T(8,128)} %select_bitcast_fusion, s32[1024]{0:T(1024)S(1)} %pad_clamp_fusion.4), kind=kCustom, calls=%fused_computation.15.clone | custom fusion | bytes 1049600 | tf_op jit(solution)/shard_map/jit(_take)/gather | solution.py:247
  217.1 4.2 %gather_fusion.11 = f32[256,512]{1,0:T(8,128)} fusion(f32[512,2048]{0,1:T(8,128)} %select_bitcast_fusion, s32[1024]{0:T(1024)S(1)} %pad_clamp_fusion.6), kind=kCustom, calls=%fused_computation.14.clone | custom fusion | bytes 1049600 | tf_op jit(solution)/shard_map/jit(_take)/gather | solution.py:247
  221.3 1.0 copy.88
  222.3 2.0 copy.85
  224.3 2.0 copy.82
  226.3 2.1 copy.79
  228.4 2.9 %fusion.6 = f32[512,256]{1,0:T(8,128)S(1)} fusion(f32[512,256]{1,0:T(8,128)S(1)} %copy-done.1, f32[256,512]{0,1:T(8,128)} %copy.88, f32[256,512]{0,1:T(8,128)S(1)} %copy.87, f32[256,512]{0,1:T(8,128)} %copy.85, f32[256,512]{0,1:T(8,128)S(1)} %copy.84, f32[256,512]{0,1:T(8,128)} %copy.82, f32[256,512]{0,1:T(8,128)S(1)} %copy.81, f32[256,512]{0,1:T(8,128)} %copy.79, ...), kind=kLoop, calls=%fused_computation.32 | loop fusion | flops 7733248 | bytes 5791744 | tf_op jit(solution)/shard_map/add | solution.py:193
  231.4 0.3 convolution_multiply_fusion.2
  231.8 38.7 %all_to_all.33 = f32[64,13,256]{2,1,0:T(8,128)S(1)} all-to-all(f32[64,13,256]{2,1,0:T(8,128)S(1)} %broadcast_in_dim.128), channel_id=1, replica_groups=mesh['space'=8,'vel'=64] {'vel'}, dimensions={0} | all-to-all | bytes 1703936 | tf_op jit(solution)/shard_map/all_to_all | solution.py:19
  270.7 1.2 stack.14
  (104 shorter events, 2.8 us)
Async XLA Ops:
  7.2 83.6 %all-gather.3.cloned.1.call-start = ((), (), s32[]{:S(2)}) async-start(), calls=%async_computation.6 | async-start | bytes 4718592 | tf_op jit(solution)/shard_map/all_gather | solution.py:233
  9.2 18.2 %copy-start = (f32[512,256]{0,1:T(8,128)S(1)}, f32[512,256]{0,1:T(8,128)}, u32[]{:S(2)}) copy-start(f32[512,256]{0,1:T(8,128)} %copy.61) | copy-start | bytes 1572868
  10.7 21.6 %all-to-all-start.2 = ((s32[8,1,8,256]{3,2,1,0:T(8,128)}), s32[8,1,8,256]{3,2,1,0:T(8,128)S(1)}, u32[]{:S(2)}, u32[]{:S(2)}) async-start(s32[8,1,8,256]{3,2,1,0:T(8,128)} %broadcast_in_dim.117), calls=%async_computation.2 | async-start | bytes 131072 | tf_op jit(solution)/shard_map/all_to_all | solution.py:19
  31.0 13.5 %copy-start.4 = (f32[4,3,256]{2,0,1:T(4,128)S(1)}, f32[4,3,256]{2,0,1:T(4,128)}, u32[]{:S(2)}) copy-start(f32[4,3,256]{2,0,1:T(4,128)} %param.12) | copy-start | bytes 36868
  33.4 39.6 %all-to-all-start = ((f32[64,13,256]{2,1,0:T(8,128)}), f32[64,13,256]{2,1,0:T(8,128)S(1)}, u32[]{:S(2)}, u32[]{:S(2)}) async-start(f32[64,13,256]{2,1,0:T(8,128)} %broadcast_in_dim.112), calls=%async_computation | async-start | bytes 2097152 | tf_op jit(solution)/shard_map/all_to_all | solution.py:19
  74.6 16.0 %all-to-all-start.1 = ((f32[64,1,256]{2,1,0:T(1,128)}), f32[64,1,256]{2,1,0:T(1,128)S(1)}, u32[]{:S(2)}, u32[]{:S(2)}) async-start(f32[64,1,256]{2,1,0:T(1,128)} %broadcast_in_dim.113), calls=%async_computation.1 | async-start | bytes 131072 | tf_op jit(solution)/shard_map/all_to_all | solution.py:19
  80.8 103.6 %all-gather.5.cloned.1.call-start = ((), (), s32[]{:S(2)}) async-start(), calls=%async_computation.7 | async-start | bytes 4718592 | tf_op jit(solution)/shard_map/all_gather | solution.py:233
  119.3 8.4 %copy-start.2 = (f32[512,256]{1,0:T(8,128)S(1)}, f32[512,256]{1,0:T(8,128)}, u32[]{:S(2)}) copy-start(f32[512,256]{1,0:T(8,128)} %param.11) | copy-start | bytes 1572868
  131.2 41.8 %copy-start.1 = (f32[512,256]{1,0:T(8,128)S(1)}, f32[512,256]{1,0:T(8,128)}, u32[]{:S(2)}) copy-start(f32[512,256]{1,0:T(8,128)} %fusion.16) | copy-start | bytes 1572868
  166.8 16.0 %all-to-all-start.4 = ((f32[64,1,256]{2,1,0:T(1,128)}), f32[64,1,256]{2,1,0:T(1,128)S(1)}, u32[]{:S(2)}, u32[]{:S(2)}) async-start(f32[64,1,256]{2,1,0:T(1,128)} %broadcast_in_dim.127), calls=%async_computation.4 | async-start | bytes 131072 | tf_op jit(solution)/shard_map/all_to_all | solution.py:19
  231.3 40.6 %copy-start.3 = (f32[512,256]{1,0:T(8,128)}, f32[512,256]{1,0:T(8,128)S(1)}, u32[]{:S(2)}) copy-start(f32[512,256]{1,0:T(8,128)S(1)} %fusion.6) | copy-start | bytes 1572868
Sparse Core Ops, SparseCore 0:
  10.7 63.7 all-gather.2
  131.4 53.0 all-gather.4
where the time goes:
time: 280 us; the launch traced here: 279 us
  local copies, waits for them, and re-layouts  95.1 us (34%)
  blocking collectives  71.1 us (25%)
  waiting for transfers between devices  39.9 us (14%)
  starting transfers between devices  34.6 us (12%)
  other arithmetic  19 us (7%)
  between operations  14.8 us (5%)
  matrix products  4.28 us (2%)
    all_to_all x2, blocking collectives, sent_to_all(): return lax.all_to_all(copies, axis, split_axis=0, concat_axis=0, tiled=True)  71.1 us
    gather x16, local copies, waits for them, and re-layouts, per_device(): jnp.take(ghosts, ghost_index[side], axis=1)  44.5 us
    all_to_all x4, waiting for transfers between devices, sent_to_all(): return lax.all_to_all(copies, axis, split_axis=0, concat_axis=0, tiled=True)  38.3 us
    all_to_all x4, starting transfers between devices, sent_to_all(): return lax.all_to_all(copies, axis, split_axis=0, concat_axis=0, tiled=True)  34.3 us
    gather x2, local copies, waits for them, and re-layouts, per_device(): ghosts = jnp.take(border, pull_index, axis=1)  23.5 us
    gather x16, local copies, waits for them, and re-layouts, per_device(): jnp.take(current, local_index[side], axis=1)  13.9 us
    select_n x2, other arithmetic, per_device(): ghosts = jnp.take(border, pull_index, axis=1)  7.53 us
    add x2, other arithmetic, relax(): current + time_step * (params[23][None, :] * (gauss - current) - outflow...  6.51 us
  transfers between devices with their start and end apart: 6, of which 4 were waited for; matrix products, arithmetic and copies ran while one was open for 10% of the time, Pallas kernels for 0%

commit v1 on v0

--- a/solution.py
+++ b/solution.py
@@ -12,6 +12,11 @@
 prandtl = 0.8
 visc_power = 0.26
 time_step = 0.025
+
+
+def tiled_gather(x, axis, dim):
+    copies = jnp.concatenate([x] * lax.axis_size(axis), axis=dim)
+    return lax.all_to_all(copies, axis, dim, dim, tiled=True)
 
 
 def sent_to_all(x, axis):
@@ -230,7 +235,7 @@
     current = distribution
     for iteration in range(ITERS):
         params = reduce_moments(current)
-        border = lax.all_gather(current, "space", axis=1, tiled=True)
+        border = tiled_gather(current, "space", 1)
         ghosts = jnp.take(border, pull_index, axis=1)
         exponent = jnp.dot(
             quad_table,

time: 280 us -> 458 us (1.64)
  waiting for transfers between devices: 39.9 us -> 229 us
  blocking collectives: 71.1 us -> 35.4 us
  local copies, waits for them, and re-layouts: 95.1 us -> 118 us
  starting transfers between devices: 34.6 us -> 54.3 us
  between operations: 14.8 us -> 1.31 us
    all_to_all x0 -> x2, waiting for transfers between devices: none -> 169 us  [tiled_gather(): return lax.all_to_all(copies, axis, dim, dim, tiled=True)]
    all_to_all x2 -> x1, blocking collectives: 71.1 us -> 35.4 us  [sent_to_all(): return lax.all_to_all(copies, axis, split_axis=0, concat_axis=0, tiled=True)]
    all_to_all x4 -> x5, waiting for transfers between devices: 38.3 us -> 59.4 us  [sent_to_all(): return lax.all_to_all(copies, axis, split_axis=0, concat_axis=0, tiled=True)]
    all_to_all x0 -> x3, local copies, waits for them, and re-layouts: none -> 15.3 us  [tiled_gather(): return lax.all_to_all(copies, axis, dim, dim, tiled=True)]
    all_to_all x0 -> x2, starting transfers between devices: none -> 11.1 us  [tiled_gather(): return lax.all_to_all(copies, axis, dim, dim, tiled=True)]
    unnamed x13 -> x28, local copies, waits for them, and re-layouts: 2.14 us -> 11.8 us
    all_to_all x4 -> x5, starting transfers between devices: 34.3 us -> 43.1 us  [sent_to_all(): return lax.all_to_all(copies, axis, split_axis=0, concat_axis=0, tiled=True)]
    all_gather x1 -> x0, local copies, waits for them, and re-layouts: 5.34 us -> none  [per_device(): border = lax.all_gather(current, 'space', axis=1, tiled=True)]
  transfers between devices with their start and end apart: 6 -> 7, of which waited for: 4 -> 7; matrix products, arithmetic and copies ran while one was open for 10% -> 10% of each run, Pallas kernels for 0% -> 0%
where the time goes in v1:
time: 458 us; the launch traced here: 456 us
  waiting for transfers between devices  229 us (50%)
  local copies, waits for them, and re-layouts  118 us (26%)
  starting transfers between devices  54.3 us (12%)
  blocking collectives  35.4 us (8%)
  other arithmetic  15.9 us (3%)
    all_to_all x2, waiting for transfers between devices, tiled_gather(): return lax.all_to_all(copies, axis, dim, dim, tiled=True)  169 us
    all_to_all x5, waiting for transfers between devices, sent_to_all(): return lax.all_to_all(copies, axis, split_axis=0, concat_axis=0, tiled=True)  59.4 us
    all_to_all x5, starting transfers between devices, sent_to_all(): return lax.all_to_all(copies, axis, split_axis=0, concat_axis=0, tiled=True)  43.1 us
    gather x16, local copies, waits for them, and re-layouts, per_device(): jnp.take(ghosts, ghost_index[side], axis=1)  40.8 us
    all_to_all x1, blocking collectives, sent_to_all(): return lax.all_to_all(copies, axis, split_axis=0, concat_axis=0, tiled=True)  35.4 us
    gather x2, local copies, waits for them, and re-layouts, per_device(): ghosts = jnp.take(border, pull_index, axis=1)  23.4 us
    gather x16, local copies, waits for them, and re-layouts, per_device(): jnp.take(current, local_index[side], axis=1)  18.4 us
    all_to_all x3, local copies, waits for them, and re-layouts, tiled_gather(): return lax.all_to_all(copies, axis, dim, dim, tiled=True)  15.3 us
  transfers between devices with their start and end apart: 7, of which 7 were waited for; matrix products, arithmetic and copies ran while one was open for 10% of the time, Pallas kernels for 0%

profile of v1, /device:TPU:1, one launch (start us, length us, event | category | flops | bytes accessed | tf_op | source)
XLA Modules:
  0.0 456.5 jit_solution(4173499744871663356)
XLA Ops:
  1.0 1.3 convolution_multiply_fusion.4
  2.4 1.1 broadcast_in_dim.112
  3.5 11.8 %all-to-all-start = ((f32[64,13,256]{2,1,0:T(8,128)}), f32[64,13,256]{2,1,0:T(8,128)S(1)}, u32[]{:S(2)}, u32[]{:S(2)}) async-start(f32[64,13,256]{2,1,0:T(8,128)} %broadcast_in_dim.112), calls=%async_computation | async-start | bytes 2097152 | tf_op jit(solution)/shard_map/all_to_all | solution.py:24
  15.3 0.9 constant_dynamic-update-slice_fusion.7
  18.0 0.9 constant_dynamic-update-slice_fusion.4
  18.9 0.9 constant_dynamic-update-slice_fusion.3
  20.6 23.2 %all-to-all-done = f32[64,13,256]{2,1,0:T(8,128)S(1)} async-done(((f32[64,13,256]{2,1,0:T(8,128)}), f32[64,13,256]{2,1,0:T(8,128)S(1)}, u32[]{:S(2)}, u32[]{:S(2)}) %all-to-all-start) | async-done | bytes 852000 | tf_op jit(solution)/shard_map/all_to_all | solution.py:24
  44.4 10.1 %all-to-all-start.3 = ((s32[8,1,8,256]{3,2,1,0:T(8,128)}), s32[8,1,8,256]{3,2,1,0:T(8,128)S(1)}, u32[]{:S(2)}, u32[]{:S(2)}) async-start(s32[8,1,8,256]{3,2,1,0:T(8,128)} %broadcast_in_dim.117), calls=%async_computation.3 | async-start | bytes 131072 | tf_op jit(solution)/shard_map/all_to_all | solution.py:24
  55.5 6.2 %all-to-all-done.3 = s32[8,1,8,256]{3,2,1,0:T(8,128)S(1)} async-done(((s32[8,1,8,256]{3,2,1,0:T(8,128)}), s32[8,1,8,256]{3,2,1,0:T(8,128)S(1)}, u32[]{:S(2)}, u32[]{:S(2)}) %all-to-all-start.3) | async-done | bytes 65568 | tf_op jit(solution)/shard_map/all_to_all | solution.py:24
  62.3 7.7 %all-to-all-start.1 = ((f32[64,1,256]{2,1,0:T(1,128)}), f32[64,1,256]{2,1,0:T(1,128)S(1)}, u32[]{:S(2)}, u32[]{:S(2)}) async-start(f32[64,1,256]{2,1,0:T(1,128)} %broadcast_in_dim.113), calls=%async_computation.1 | async-start | bytes 131072 | tf_op jit(solution)/shard_map/all_to_all | solution.py:24
  70.0 0.9 constant_dynamic-update-slice_fusion.1
  70.9 0.9 constant_dynamic-update-slice_fusion
  71.8 5.4 %copy.119 = f32[512,2048]{0,1:T(8,128)} copy(f32[512,2048]{1,0:T(8,128)} %constant_dynamic-update-slice_fusion) | data formatting | bytes 8388608 | tf_op jit(solution)/shard_map/all_to_all | solution.py:19
  77.2 2.6 all-to-all-done.1
  79.8 4.9 %all-to-all-start.2 = ((f32[512,8,256]{0,2,1:T(8,128)}), f32[512,8,256]{0,2,1:T(8,128)}, u32[]{:S(2)}, u32[]{:S(2)}) async-start(f32[512,8,256]{0,2,1:T(8,128)} %bitcast.150), calls=%async_computation.2 | async-start | bytes 8388608 | tf_op jit(solution)/shard_map/all_to_all | solution.py:19
  85.4 1.0 gather_fusion.7
  86.6 1.0 gather_fusion.5
  87.9 1.8 gather_fusion.3
  89.6 1.2 copy.94
  90.9 1.8 gather_fusion
  92.7 2.1 copy.90
  95.1 81.9 %all-to-all-done.2 = f32[512,8,256]{0,2,1:T(8,128)} async-done(((f32[512,8,256]{0,2,1:T(8,128)}), f32[512,8,256]{0,2,1:T(8,128)}, u32[]{:S(2)}, u32[]{:S(2)}) %all-to-all-start.2) | async-done | bytes 4194336 | tf_op jit(solution)/shard_map/all_to_all | solution.py:19
  177.0 11.7 %gather_fusion.1 = f32[2048,512]{1,0:T(8,128)} fusion(f32[512,2048]{0,1:T(8,128)} %bitcast.22, s32[2048]{0:T(1024)S(1)} %broadcast_clamp_fusion), kind=kCustom, calls=%fused_computation.1.clone | custom fusion | bytes 8396800 | tf_op jit(solution)/shard_map/jit(_take)/gather | solution.py:239
  188.8 3.8 select_bitcast_fusion.1
  192.6 3.4 gather_fusion.8
  196.0 1.0 copy.101
  197.0 3.4 gather_fusion.6
  200.4 1.0 copy.98
  201.4 3.4 gather_fusion.4
  204.8 1.0 copy.95
  205.8 3.4 gather_fusion.2
  209.2 1.0 copy.92
  210.2 3.8 constant_dynamic-update-slice_fusion.15
  214.3 1.1 broadcast_in_dim.126
  215.4 7.5 %all-to-all-start.4 = ((f32[64,13,256]{2,1,0:T(8,128)}), f32[64,13,256]{2,1,0:T(8,128)S(1)}, u32[]{:S(2)}, u32[]{:S(2)}) async-start(f32[64,13,256]{2,1,0:T(8,128)} %broadcast_in_dim.126), calls=%async_computation.4 | async-start | bytes 2097152 | tf_op jit(solution)/shard_map/all_to_all | solution.py:24
  225.5 0.9 constant_dynamic-update-slice_fusion.11
  227.3 24.2 %all-to-all-done.4 = f32[64,13,256]{2,1,0:T(8,128)S(1)} async-done(((f32[64,13,256]{2,1,0:T(8,128)}), f32[64,13,256]{2,1,0:T(8,128)S(1)}, u32[]{:S(2)}, u32[]{:S(2)}) %all-to-all-start.4) | async-done | bytes 852000 | tf_op jit(solution)/shard_map/all_to_all | solution.py:24
  253.1 6.2 %all-to-all-start.5 = ((f32[64,1,256]{2,1,0:T(1,128)}), f32[64,1,256]{2,1,0:T(1,128)S(1)}, u32[]{:S(2)}, u32[]{:S(2)}) async-start(f32[64,1,256]{2,1,0:T(1,128)} %broadcast_in_dim.127), calls=%async_computation.5 | async-start | bytes 131072 | tf_op jit(solution)/shard_map/all_to_all | solution.py:24
  259.3 0.9 constant_dynamic-update-slice_fusion.9
  260.2 0.9 constant_dynamic-update-slice_fusion.8
  261.1 4.6 %copy.144 = f32[64,8,8,256]{3,2,0,1:T(8,128)} copy(f32[64,8,8,256]{3,2,1,0:T(8,128)} %bitcast.152) | data formatting | bytes 8388608 | tf_op jit(solution)/shard_map/all_to_all | solution.py:19
  265.7 3.4 all-to-all-done.5
  269.1 6.2 %all-to-all-start.6 = ((f32[512,8,256]{2,0,1:T(8,128)}), f32[512,8,256]{2,0,1:T(8,128)}, u32[]{:S(2)}, u32[]{:S(2)}) async-start(f32[512,8,256]{2,0,1:T(8,128)} %bitcast.151), calls=%async_computation.6 | async-start | bytes 8388608 | tf_op jit(solution)/shard_map/all_to_all | solution.py:19
  275.5 1.0 gather_fusion.16
  276.5 1.0 gather_fusion.14
  277.5 1.8 gather_fusion.12
  279.2 1.8 gather_fusion.9
  281.4 1.2 copy.110
  282.7 2.1 copy.105
  284.9 87.4 %all-to-all-done.6 = f32[512,8,256]{2,0,1:T(8,128)} async-done(((f32[512,8,256]{2,0,1:T(8,128)}), f32[512,8,256]{2,0,1:T(8,128)}, u32[]{:S(2)}, u32[]{:S(2)}) %all-to-all-start.6) | async-done | bytes 4194336 | tf_op jit(solution)/shard_map/all_to_all | solution.py:19
  372.3 5.4 %copy.107 = f32[512,8,256]{0,2,1:T(8,128)} copy(f32[512,8,256]{2,0,1:T(8,128)} %all-to-all-done.6) | data formatting | bytes 8388608 | tf_op jit(solution)/shard_map/all_to_all | solution.py:19
  377.6 11.7 %gather_fusion.10 = f32[2048,512]{1,0:T(8,128)} fusion(f32[512,2048]{0,1:T(8,128)} %bitcast.149, s32[2048]{0:T(1024)S(1)} %broadcast_clamp_fusion), kind=kCustom, calls=%fused_computation.10.clone | custom fusion | bytes 8396800 | tf_op jit(solution)/shard_map/jit(_take)/gather | solution.py:239
  389.3 3.8 select_bitcast_fusion
  393.1 3.4 gather_fusion.17
  396.5 4.2 gather_fusion.15
  400.7 4.2 gather_fusion.13
  404.9 4.2 gather_fusion.11
  409.1 1.0 copy.117
  410.1 2.0 copy.114
  412.1 2.1 copy.111
  414.2 2.0 copy.108
  416.2 2.9 fusion.6
  419.6 35.4 %all_to_all.56 = f32[64,13,256]{2,1,0:T(8,128)S(1)} all-to-all(f32[64,13,256]{2,1,0:T(8,128)S(1)} %broadcast_in_dim.128), channel_id=1, replica_groups=mesh['space'=8,'vel'=64] {'vel'}, dimensions={0} | all-to-all | bytes 1703936 | tf_op jit(solution)/shard_map/all_to_all | solution.py:24
  455.2 1.2 stack.14
  (115 shorter events, 13.2 us)
Async XLA Ops:
  0.6 14.7 %copy-start = (f32[512,256]{1,0:T(8,128)S(1)}, f32[512,256]{1,0:T(8,128)}, u32[]{:S(2)}) copy-start(f32[512,256]{1,0:T(8,128)} %param.11) | copy-start | bytes 1572868
  3.5 40.3 %copy-start.4 = (s32[1,8,256]{2,1,0:T(8,128)S(1)}, s32[1,8,256]{2,1,0:T(8,128)}, u32[]{:S(2)}) copy-start(s32[1,8,256]{2,1,0:T(8,128)} %param.14) | copy-start | bytes 24580
  3.5 40.3 %all-to-all-start = ((f32[64,13,256]{2,1,0:T(8,128)}), f32[64,13,256]{2,1,0:T(8,128)S(1)}, u32[]{:S(2)}, u32[]{:S(2)}) async-start(f32[64,13,256]{2,1,0:T(8,128)} %broadcast_in_dim.112), calls=%async_computation | async-start | bytes 2097152 | tf_op jit(solution)/shard_map/all_to_all | solution.py:24
  44.4 17.2 %all-to-all-start.3 = ((s32[8,1,8,256]{3,2,1,0:T(8,128)}), s32[8,1,8,256]{3,2,1,0:T(8,128)S(1)}, u32[]{:S(2)}, u32[]{:S(2)}) async-start(s32[8,1,8,256]{3,2,1,0:T(8,128)} %broadcast_in_dim.117), calls=%async_computation.3 | async-start | bytes 131072 | tf_op jit(solution)/shard_map/all_to_all | solution.py:24
  62.3 17.5 %all-to-all-start.1 = ((f32[64,1,256]{2,1,0:T(1,128)}), f32[64,1,256]{2,1,0:T(1,128)S(1)}, u32[]{:S(2)}, u32[]{:S(2)}) async-start(f32[64,1,256]{2,1,0:T(1,128)} %broadcast_in_dim.113), calls=%async_computation.1 | async-start | bytes 131072 | tf_op jit(solution)/shard_map/all_to_all | solution.py:24
  79.8 5.2 %copy-start.5 = (s32[8,1]{0,1:T(1,128)S(1)}, s32[8,1]{0,1:T(1,128)}, u32[]{:S(2)}) copy-start(s32[8,1]{0,1:T(1,128)} %param.15) | copy-start | bytes 100
  79.8 5.4 %copy-start.2 = (s32[4,256]{1,0:T(4,128)S(1)}, s32[4,256]{1,0:T(4,128)}, u32[]{:S(2)}) copy-start(s32[4,256]{1,0:T(4,128)} %param.13) | copy-start | bytes 12292
  79.8 97.2 %all-to-all-start.2 = ((f32[512,8,256]{0,2,1:T(8,128)}), f32[512,8,256]{0,2,1:T(8,128)}, u32[]{:S(2)}, u32[]{:S(2)}) async-start(f32[512,8,256]{0,2,1:T(8,128)} %bitcast.150), calls=%async_computation.2 | async-start | bytes 8388608 | tf_op jit(solution)/shard_map/all_to_all | solution.py:19
  89.6 5.3 %copy-start.3 = (f32[4,3,256]{2,0,1:T(4,128)S(1)}, f32[4,3,256]{2,0,1:T(4,128)}, u32[]{:S(2)}) copy-start(f32[4,3,256]{2,0,1:T(4,128)} %param.12) | copy-start | bytes 36868
  215.4 36.0 %all-to-all-start.4 = ((f32[64,13,256]{2,1,0:T(8,128)}), f32[64,13,256]{2,1,0:T(8,128)S(1)}, u32[]{:S(2)}, u32[]{:S(2)}) async-start(f32[64,13,256]{2,1,0:T(8,128)} %broadcast_in_dim.126), calls=%async_computation.4 | async-start | bytes 2097152 | tf_op jit(solution)/shard_map/all_to_all | solution.py:24
  253.1 16.0 %all-to-all-start.5 = ((f32[64,1,256]{2,1,0:T(1,128)}), f32[64,1,256]{2,1,0:T(1,128)S(1)}, u32[]{:S(2)}, u32[]{:S(2)}) async-start(f32[64,1,256]{2,1,0:T(1,128)} %broadcast_in_dim.127), calls=%async_computation.5 | async-start | bytes 131072 | tf_op jit(solution)/shard_map/all_to_all | solution.py:24
  269.1 103.2 %all-to-all-start.6 = ((f32[512,8,256]{2,0,1:T(8,128)}), f32[512,8,256]{2,0,1:T(8,128)}, u32[]{:S(2)}, u32[]{:S(2)}) async-start(f32[512,8,256]{2,0,1:T(8,128)} %bitcast.151), calls=%async_computation.6 | async-start | bytes 8388608 | tf_op jit(solution)/shard_map/all_to_all | solution.py:19
  419.1 37.3 %copy-start.1 = (f32[512,256]{1,0:T(8,128)}, f32[512,256]{1,0:T(8,128)S(1)}, u32[]{:S(2)}) copy-start(f32[512,256]{1,0:T(8,128)S(1)} %fusion.6) | copy-start | bytes 1572868
